TPU v7x, 256 devices: a whole 4x4x8 slice. The times are simulated.
256 devices in a mesh: seq: 8 (over y, core), ep: 32 (over x, z).
Axes of the slice: x: 4, y: 4, z: 8, core: 2. Of those that a mesh axis runs over, the one named last changes fastest.
Arguments:
- entering: bfloat16 [32, 32, 7168], P('ep', 'seq'), may hold values from -6 to 6
- moe_gain: float32 [7168], replicated, may hold values from 0.1 to 1.9
- expert_ids: int32 [32, 32, 8], P('ep'), may hold values from 0 to 31, all different within a row; in each aligned block of 4 rows (0 to 3, 4 to 7, ..., all dimensions but the last counted through in order) at most 2 rows name the same one
- gate_weights: float32 [32, 32, 8], P('ep'), may hold values from 0.05 to 0.5
- w_gate: bfloat16 [32, 7168, 2048], P('ep', None, 'seq'), may hold values from -0.0625 to 0.0625
- w_up: bfloat16 [32, 7168, 2048], P('ep', None, 'seq'), may hold values from -0.0625 to 0.0625
- w_down: bfloat16 [32, 2048, 7168], P('ep', 'seq'), may hold values from -0.125 to 0.125
- w_latent: bfloat16 [7168, 512], P('seq'), may hold values from -0.0625 to 0.0625
- w_rope: bfloat16 [64, 7168], P(None, 'seq'), may hold values from -0.0625 to 0.0625
- latent_gain: float32 [512], replicated, may hold values from 0.1 to 1.9
- prefix_len: int32 [32], P('ep'), may hold values from 128 to 1024, as said below
- cache_latent: bfloat16 [32, 1024, 512], P('ep', 'seq'), may hold values from -4 to 4
- cache_rope: bfloat16 [32, 64, 1024], P('ep', None, 'seq'), may hold values from -4 to 4
- query_latent: bfloat16 [32, 32, 65536], P('ep', 'seq'), may hold values from -7 to 7
- query_rope: bfloat16 [32, 32, 8192], P('ep', 'seq'), may hold values from -32 to 32
Outputs:
- layer_out: bfloat16 [32, 32, 7168], P('ep', None, 'seq')
- attention: bfloat16 [32, 32, 65536], P('ep', 'seq')
Inputs may be any that keep to these rules, and one draw needn't show every extreme that they name: `expert_ids`: in each aligned block of 4 rows (one document's new tokens on one index of seq) no expert is named by more than 2 tokens, and in some blocks one is named by exactly 2. Each token names 8 different experts. `prefix_len`: some document has all 1024 positions cached.
All inputs are finite; a program needn't handle non-finite values.
Results may differ from a plain program's by a relative error of at most 0.018.
Values may be sent and summed in bfloat16 or wider, within the bound.
A program may use at most 128 MiB of HBM per device.

v0:
```python
import jax
import jax.numpy as jnp
from jax import lax
from jax.sharding import PartitionSpec as P

softmax_scale = 192 ** (-0.5)
rope_base = 10000.0


def rms_rows(values, gain):
    mean_sq = jnp.mean(values * values, axis=-1, keepdims=True)
    return values * lax.rsqrt(mean_sq + 1e-06) * gain


def rotate_pairs(values, positions):
    half = values.shape[-1] // 2
    steps = jnp.arange(half, dtype=jnp.float32) * 2.0 / values.shape[-1]
    freqs = rope_base ** (-steps)
    angle = positions.astype(jnp.float32)[:, None] * freqs[None, :]
    first = values[:, :half]
    second = values[:, half:]
    cosine = jnp.cos(angle)
    sine = jnp.sin(angle)
    return jnp.concatenate(
        [first * cosine - second * sine, second * cosine + first * sine], axis=-1
    )


def score_block(query_lat, query_rot, key_lat, key_rot_cols):
    lat_part = jnp.dot(query_lat, key_lat.T, preferred_element_type=jnp.float32)
    rot_part = jnp.dot(query_rot, key_rot_cols, preferred_element_type=jnp.float32)
    return (lat_part + rot_part) * softmax_scale


def block_slots(routes, experts, capacity):
    same = (routes[:, :, None, None] == routes[None, None, :, :]).any(axis=3)
    order = jnp.arange(routes.shape[0], dtype=jnp.int32)
    earlier = order[None, :] < order[:, None]
    slots = jnp.sum((same & earlier[:, None, :]).astype(jnp.int32), axis=2)
    return routes * capacity + slots


def expert_terms(rows, gate_matrix, up_matrix, down_matrix):
    gate = jnp.dot(rows, gate_matrix, preferred_element_type=jnp.float32)
    upper = jnp.dot(rows, up_matrix, preferred_element_type=jnp.float32)
    hidden = (jax.nn.silu(gate) * upper).astype(jnp.bfloat16)
    return jnp.dot(hidden, down_matrix, preferred_element_type=jnp.float32)


def local(
    entering,
    moe_gain,
    expert_ids,
    gate_weights,
    w_gate,
    w_up,
    w_down,
    w_latent,
    w_rope,
    latent_gain,
    prefix_len,
    cache_latent,
    cache_rope,
    query_latent,
    query_rope,
):
    seq_count = lax.axis_size("seq")
    seq_place = lax.axis_index("seq")
    experts = lax.axis_size("ep")
    own_entering = entering[0]
    new_dev, width = own_entering.shape
    new = new_dev * seq_count
    capacity = 2
    prefix = prefix_len[0]
    heads = query_latent.shape[2] // cache_latent.shape[2]
    lat_width = cache_latent.shape[2]
    rot_width = cache_rope.shape[1]
    routes = lax.dynamic_slice_in_dim(expert_ids[0], seq_place * new_dev, new_dev, 0)
    gates = lax.dynamic_slice_in_dim(gate_weights[0], seq_place * new_dev, new_dev, 0)
    normed = rms_rows(own_entering.astype(jnp.float32), moe_gain).astype(jnp.bfloat16)
    targets = block_slots(routes, experts, capacity)
    total_slots = experts * capacity
    hits = targets[:, :, None] == jnp.arange(total_slots, dtype=jnp.int32)[None, None, :]
    placement = jnp.any(hits, axis=1).astype(jnp.bfloat16)
    gate_rows = jnp.sum(jnp.where(hits, gates[:, :, None], 0.0), axis=1)
    outgoing = jnp.dot(placement.T, normed, preferred_element_type=jnp.float32)
    outgoing = outgoing.astype(jnp.bfloat16).reshape(experts, capacity, width)
    arrived = lax.all_to_all(outgoing, "ep", split_axis=0, concat_axis=0, tiled=True)
    rows = lax.all_gather(arrived.reshape(total_slots, width), "seq", axis=0, tiled=True)
    older_lat = lax.all_gather(cache_latent[0], "seq", axis=0, tiled=True)
    older_rot = lax.all_gather(cache_rope[0], "seq", axis=1, tiled=True)
    query_lat = query_latent[0].reshape(new_dev * heads, lat_width)
    query_rot = query_rope[0].reshape(new_dev * heads, rot_width)
    older = score_block(query_lat, query_rot, older_lat, older_rot)
    cache_ok = (jnp.arange(older_lat.shape[0], dtype=jnp.int32) < prefix)[None, :]
    older = jnp.where(cache_ok, older, -jnp.inf)
    older_high = jnp.max(older, axis=1)
    older_weights = jnp.exp(older - older_high[:, None])
    older_total = jnp.sum(older_weights, axis=1)
    older_sum = jnp.dot(
        older_weights.astype(jnp.bfloat16), older_lat, preferred_element_type=jnp.float32
    )
    terms = expert_terms(rows, w_gate[0], w_up[0], w_down[0]).astype(jnp.bfloat16)
    summed = lax.psum_scatter(terms, "seq", scatter_dimension=0, tiled=True)
    summed = summed.reshape(experts, capacity, width)
    returned = lax.all_to_all(summed, "ep", split_axis=0, concat_axis=0, tiled=True)
    weighted = jnp.dot(
        gate_rows,
        returned.reshape(total_slots, width).astype(jnp.float32),
        precision=lax.Precision.HIGHEST,
    )
    layer_own = (own_entering.astype(jnp.float32) + weighted).astype(jnp.bfloat16)
    layer = lax.all_to_all(layer_own, "seq", split_axis=1, concat_axis=0, tiled=True)
    latent_part = jnp.dot(layer, w_latent, preferred_element_type=jnp.float32)
    rope_part = lax.dot_general(
        layer, w_rope, (((1,), (1,)), ((), ())), preferred_element_type=jnp.float32
    )
    raw = lax.psum(jnp.concatenate([latent_part, rope_part], axis=1), "seq")
    fresh_lat = rms_rows(raw[:, :lat_width], latent_gain).astype(jnp.bfloat16)
    positions = prefix + jnp.arange(new, dtype=jnp.int32)
    fresh_rot = rotate_pairs(raw[:, lat_width:], positions).astype(jnp.bfloat16)
    fresh = score_block(query_lat, query_rot, fresh_lat, fresh_rot.T)
    query_place = seq_place * new_dev + jnp.arange(new_dev * heads, dtype=jnp.int32) // heads
    fresh_ok = jnp.arange(new, dtype=jnp.int32)[None, :] <= query_place[:, None]
    fresh = jnp.where(fresh_ok, fresh, -jnp.inf)
    highest = jnp.maximum(older_high, jnp.max(fresh, axis=1))
    scale = jnp.exp(older_high - highest)
    fresh_weights = jnp.exp(fresh - highest[:, None])
    total = older_total * scale + jnp.sum(fresh_weights, axis=1)
    gathered = older_sum * scale[:, None] + jnp.dot(
        fresh_weights.astype(jnp.bfloat16), fresh_lat, preferred_element_type=jnp.float32
    )
    output = (gathered / total[:, None]).astype(jnp.bfloat16).reshape(new_dev, heads * lat_width)
    return (layer[None], output[None])


def solution(mesh):
    placed = (
        P("ep", "seq", None),
        P(),
        P("ep", None, None),
        P("ep", None, None),
        P("ep", None, "seq"),
        P("ep", None, "seq"),
        P("ep", "seq", None),
        P("seq", None),
        P(None, "seq"),
        P(),
        P("ep"),
        P("ep", "seq", None),
        P("ep", None, "seq"),
        P("ep", "seq", None),
        P("ep", "seq", None),
    )
    return jax.shard_map(
        local,
        mesh=mesh,
        in_specs=placed,
        out_specs=(P("ep", None, "seq"), P("ep", "seq", None)),
        check_vma=False,
    )
```

profile of v0, /device:TPU:1, one launch (start us, length us, event | category | flops | bytes accessed | tf_op | source)
XLA Modules:
  0.0 291.2 jit_solution(7209616721143365374)
XLA Ops:
  7.2 0.8 constant_dynamic-slice_fusion.1
  8.1 0.1 copy.23
  8.2 0.4 compare_reduce_fusion
  8.6 0.1 convert_reduce_fusion
  8.7 0.1 fusion.47
  8.8 1.0 fusion.28
  9.8 1.3 convolution_convert_fusion.1
  11.1 0.3 reshape.118
  11.4 33.6 %all_to_all.29 = bf16[32,2,7168]{2,1,0:T(2,128)(2,1)S(1)} all-to-all(bf16[32,2,7168]{2,1,0:T(2,128)(2,1)S(1)} %reshape.118), channel_id=1, replica_groups=mesh['seq'=8,'ep'=32] {'ep'}, dimensions={0} | all-to-all | bytes 1835008 | tf_op jit(solution)/shard_map/all_to_all | solution.py:88
  45.0 1.3 reshape.119
  46.3 0.0 reduce-scatter.2.cloned.1.call-start
  46.4 49.3 %all-gather.5.cloned.1.call-done = bf16[512,7168]{1,0:T(8,128)(2,1)} async-done(((bf16[64,7168]{1,0:T(8,128)(2,1)}), bf16[512,7168]{1,0:T(8,128)(2,1)}) %all-gather.5.cloned.1.call-update) | async-done | bytes 7340048 | tf_op jit(solution)/shard_map/all_gather | solution.py:89
  95.7 6.2 %fusion.4 = f32[512,256]{1,0:T(8,128)S(1)} fusion(bf16[512,7168]{1,0:T(8,128)(2,1)} %all-gather.5.cloned.1.call-done, bf16[1,7168,256]{2,1,0:T(8,128)(2,1)} %param.19), kind=kOutput, calls=%fused_computation.7 | convolution fusion | flops 1879048192 | bytes 11534336 | tf_op jit(solution)/shard_map/dot_general | solution.py:44
  101.9 16.0 %convolution_convert_fusion = bf16[512,7168]{1,0:T(8,128)(2,1)} fusion(bf16[1,256,7168]{2,1,0:T(8,128)(2,1)} %param.21, bf16[512,7168]{1,0:T(8,128)(2,1)} %all-gather.5.cloned.1.call-done, bf16[1,7168,256]{2,1,0:T(8,128)(2,1)} %param.20, f32[512,256]{1,0:T(8,128)S(1)} %fusion.4), kind=kOutput, calls=%fused_computation | convolution fusion | flops 3762552832 | bytes 22544384 | tf_op jit(solution)/shard_map/dot_general | solution.py:47
  118.0 49.3 %reduce-scatter.2.cloned.1.call-done = bf16[64,7168]{1,0:T(8,128)(2,1)} async-done(((bf16[512,7168]{1,0:T(8,128)(2,1)}), bf16[64,7168]{1,0:T(8,128)(2,1)}) %reduce-scatter.2.cloned.1.call-update) | async-done | bytes 917520 | tf_op jit(solution)/shard_map/reduce_scatter | solution.py:104
  167.2 3.1 %reshape.120 = bf16[32,2,7168]{2,1,0:T(2,128)(2,1)} reshape(bf16[64,7168]{1,0:T(8,128)(2,1)} %reduce-scatter.2.cloned.1.call-done) | data formatting | bytes 1835008 | tf_op jit(solution)/shard_map/reshape | solution.py:105
  170.3 9.7 %all-to-all-start.1 = ((bf16[32,2,7168]{2,1,0:T(2,128)(2,1)}), bf16[32,2,7168]{2,1,0:T(2,128)(2,1)S(1)}, u32[]{:S(2)}, u32[]{:S(2)}) async-start(bf16[32,2,7168]{2,1,0:T(2,128)(2,1)} %reshape.120), calls=%async_computation.2 | async-start | bytes 1835008 | tf_op jit(solution)/shard_map/all_to_all | solution.py:106
  180.0 0.2 all-gather.7.cloned.1.call-start
  180.2 0.5 all-gather.7.cloned.1.call-update
  180.7 0.1 constant_dynamic-slice_fusion
  180.8 0.1 copy.24
  180.9 0.2 reshape_squeeze.7
  181.1 0.4 reshape_squeeze.6
  182.2 12.7 %all-gather.1 = bf16[1,64,1024]{2,1,0:T(8,128)(2,1)S(1)} all-gather(bf16[1,64,128]{2,1,0:T(8,128)(2,1)S(1)} %copy-done.6), channel_id=3, replica_groups=mesh['seq'=8,'ep'=32] {'seq'}, dimensions={2}, use_global_device_ids=true | all-gather | bytes 147456 | tf_op jit(solution)/shard_map/all_gather | solution.py:91
  194.8 0.6 negate_power_fusion
  195.4 0.5 add_convert_fusion
  196.0 0.1 select_reduce_fusion
  196.1 1.8 fusion.26
  197.8 4.2 %all-to-all-done.1 = bf16[32,2,7168]{2,1,0:T(2,128)(2,1)S(1)} async-done(((bf16[32,2,7168]{2,1,0:T(2,128)(2,1)}), bf16[32,2,7168]{2,1,0:T(2,128)(2,1)S(1)}, u32[]{:S(2)}, u32[]{:S(2)}) %all-to-all-start.1) | async-done | bytes 917536 | tf_op jit(solution)/shard_map/all_to_all | solution.py:106
  202.0 0.3 reshape.121
  202.4 1.1 fusion
  203.5 8.9 %all-to-all-start.2 = ((bf16[4,8,896]{2,0,1:T(4,128)(2,1)}), bf16[4,8,896]{2,0,1:T(4,128)(2,1)}, u32[]{:S(2)}, u32[]{:S(2)}) async-start(bf16[4,8,896]{2,0,1:T(4,128)(2,1)} %bitcast.7), calls=%async_computation.3 | async-start | bytes 114688 | tf_op jit(solution)/shard_map/all_to_all | solution.py:113
  212.4 2.8 fusion.58
  215.2 2.1 all-to-all-done.2
  217.3 1.5 all_to_all.25
  218.8 1.1 fusion.61
  219.9 1.1 fusion.60
  220.9 0.7 pad_maximum_fusion
  221.6 0.5 fusion.6
  222.1 1.5 broadcast_in_dim.34
  223.5 53.4 %all-reduce.2.cloned.1.call-done = f32[32,576]{1,0:T(8,128)} async-done(((f32[32,576]{1,0:T(8,128)}), f32[32,576]{1,0:T(8,128)}) %all-reduce.2.cloned.1.call-update) | async-done | bytes 73744 | tf_op jit(solution)/shard_map/psum | solution.py:118
  276.9 1.0 multiply_reduce_fusion
  278.0 1.1 fusion.57
  279.0 1.0 fusion.44
  280.0 1.1 fusion.59
  281.2 2.0 convolution_multiply_fusion
  283.2 0.3 fusion.9
  283.5 1.2 broadcast_in_dim_reshape.3
  (33 shorter events, 0.3 us)
Async XLA Ops:
  7.2 212.7 %copy-start = (bf16[896,512]{1,0:T(8,128)(2,1)S(1)}, bf16[896,512]{1,0:T(8,128)(2,1)}, u32[]{:S(2)}) copy-start(bf16[896,512]{1,0:T(8,128)(2,1)} %param.22) | copy-start | bytes 2752516
  7.2 88.5 %all-gather.5.cloned.1.call-start = ((), (), s32[]{:S(2)}) async-start(), calls=%async_computation.4 | async-start | bytes 8257536 | tf_op jit(solution)/shard_map/all_gather | solution.py:89
  46.3 120.9 %reduce-scatter.2.cloned.1.call-start = ((), (), s32[]{:S(2)}) async-start(), calls=%async_computation.5 | async-start | bytes 8257536 | tf_op jit(solution)/shard_map/reduce_scatter | solution.py:104
  117.9 62.8 %copy-start.7 = (f32[1,32,8]{1,2,0:T(8,128)S(1)}, f32[1,32,8]{1,2,0:T(8,128)}, u32[]{:S(2)}) copy-start(f32[1,32,8]{1,2,0:T(8,128)} %param.18) | copy-start | bytes 3076
  117.9 63.0 %copy-start.5 = (bf16[1,4,8192]{2,1,0:T(4,128)(2,1)S(1)}, bf16[1,4,8192]{2,1,0:T(4,128)(2,1)}, u32[]{:S(2)}) copy-start(bf16[1,4,8192]{2,1,0:T(4,128)(2,1)} %param.29) | copy-start | bytes 196612
  117.9 63.1 %copy-start.2 = (bf16[1,4,65536]{2,1,0:T(4,128)(2,1)S(1)}, bf16[1,4,65536]{2,1,0:T(4,128)(2,1)}, u32[]{:S(2)}) copy-start(bf16[1,4,65536]{2,1,0:T(4,128)(2,1)} %param.28) | copy-start | bytes 1572868
  118.0 64.2 %copy-start.6 = (bf16[1,64,128]{2,1,0:T(8,128)(2,1)S(1)}, bf16[1,64,128]{2,1,0:T(8,128)(2,1)}, u32[]{:S(2)}) copy-start(bf16[1,64,128]{2,1,0:T(8,128)(2,1)} %param.27) | copy-start | bytes 49156
  170.3 32.1 %copy-start.3 = (bf16[1,4,7168]{2,1,0:T(4,128)(2,1)S(1)}, bf16[1,4,7168]{2,1,0:T(4,128)(2,1)}, u32[]{:S(2)}) copy-start(bf16[1,4,7168]{2,1,0:T(4,128)(2,1)} %param.15) | copy-start | bytes 172036
  170.3 31.7 %all-to-all-start.1 = ((bf16[32,2,7168]{2,1,0:T(2,128)(2,1)}), bf16[32,2,7168]{2,1,0:T(2,128)(2,1)S(1)}, u32[]{:S(2)}, u32[]{:S(2)}) async-start(bf16[32,2,7168]{2,1,0:T(2,128)(2,1)} %reshape.120), calls=%async_computation.2 | async-start | bytes 1835008 | tf_op jit(solution)/shard_map/all_to_all | solution.py:106
  180.0 32.4 %all-gather.7.cloned.1.call-start = ((), (), s32[]{:S(2)}) async-start(), calls=%async_computation.7 | async-start | bytes 1179648 | tf_op jit(solution)/shard_map/all_gather | solution.py:90
  181.1 16.8 %copy-start.1 = (bf16[512,64]{1,0:T(8,128)(2,1)}, bf16[512,64]{1,0:T(8,128)(2,1)S(1)}, u32[]{:S(2)}) copy-start(bf16[512,64]{1,0:T(8,128)(2,1)S(1)} %reshape_squeeze.7) | copy-start | bytes 196612
  203.5 13.8 %all-to-all-start.2 = ((bf16[4,8,896]{2,0,1:T(4,128)(2,1)}), bf16[4,8,896]{2,0,1:T(4,128)(2,1)}, u32[]{:S(2)}, u32[]{:S(2)}) async-start(bf16[4,8,896]{2,0,1:T(4,128)(2,1)} %bitcast.7), calls=%async_computation.3 | async-start | bytes 114688 | tf_op jit(solution)/shard_map/all_to_all | solution.py:113
  212.4 65.6 %copy-start.8 = (f32[512]{0:T(512)S(1)}, f32[512]{0:T(512)}, u32[]{:S(2)}) copy-start(f32[512]{0:T(512)} %param.24) | copy-start | bytes 6148
  212.4 64.5 %all-reduce.2.cloned.1.call-start = ((), (), s32[]{:S(2)}) async-start(), calls=%async_computation.6 | async-start | bytes 163840 | tf_op jit(solution)/shard_map/psum | solution.py:118
  276.9 6.3 %copy-start.4 = (f32[32,576]{1,0:T(8,128)S(1)}, f32[32,576]{1,0:T(8,128)}, u32[]{:S(2)}) copy-start(f32[32,576]{1,0:T(8,128)} %all-reduce.2.cloned.1.call-done) | copy-start | bytes 221188
Sparse Core Ops, SparseCore 0:
  46.5 49.1 all-gather.4
  118.0 49.1 reduce-scatter.1
  182.7 26.2 all-gather.6
  221.7 55.1 all-reduce.1
where the time goes:
time: 292 us; the launch traced here: 291 us
  waiting for transfers between devices  159 us (54%)
  blocking collectives  46.3 us (16%)
  matrix products  35.8 us (12%)
  starting transfers between devices  18.9 us (6%)
  between operations  14.6 us (5%)
  local copies, waits for them, and re-layouts  10.8 us (4%)
  other arithmetic  6.02 us (2%)
    psum x1, waiting for transfers between devices, local(): raw = lax.psum(jnp.concatenate([latent_part, rope_part], axis=1), 'seq')  53.4 us
    all_gather x1, waiting for transfers between devices, local(): lax.all_gather(arrived.reshape(total_slots, width), 'seq', axis=0, tiled=...  49.3 us
    reduce_scatter x1, waiting for transfers between devices, local(): summed = lax.psum_scatter(terms, 'seq', scatter_dimension=0, tiled=True)  49.3 us
    all_to_all x1, blocking collectives, local(): lax.all_to_all(outgoing, 'ep', split_axis=0, concat_axis=0, tiled=True)  33.6 us
    dot_general x1, matrix products, expert_terms(): return jnp.dot(hidden, down_matrix, preferred_element_type=jnp.float32)  16 us
    all_gather x1, blocking collectives, local(): older_rot = lax.all_gather(cache_rope[0], 'seq', axis=1, tiled=True)  12.7 us
    all_to_all x1, starting transfers between devices, local(): lax.all_to_all(summed, 'ep', split_axis=0, concat_axis=0, tiled=True)  9.67 us
    all_to_all x1, starting transfers between devices, local(): lax.all_to_all(layer_own, 'seq', split_axis=1, concat_axis=0, tiled=True)  8.91 us
  transfers between devices with their start and end apart: 6, of which 5 were waited for; matrix products, arithmetic and copies ran while one was open for 3% of the time, Pallas kernels for 0%

commit v1 on v0

--- a/solution.py
+++ b/solution.py
@@ -110,7 +110,10 @@
         precision=lax.Precision.HIGHEST,
     )
     layer_own = (own_entering.astype(jnp.float32) + weighted).astype(jnp.bfloat16)
-    layer = lax.all_to_all(layer_own, "seq", split_axis=1, concat_axis=0, tiled=True)
+    n_dev = lax.axis_size("seq")
+    blocks = jnp.stack(jnp.split(layer_own, n_dev, axis=1), axis=0)
+    blocks = lax.all_to_all(blocks, "seq", split_axis=0, concat_axis=0)
+    layer = jnp.concatenate(blocks, axis=0)
     latent_part = jnp.dot(layer, w_latent, preferred_element_type=jnp.float32)
     rope_part = lax.dot_general(
         layer, w_rope, (((1,), (1,)), ((), ())), preferred_element_type=jnp.float32

time: 292 us -> 296 us (1.014)
  local copies, waits for them, and re-layouts: 10.8 us -> 15.6 us
    unnamed x18 -> x25, local copies, waits for them, and re-layouts: 0.06 us -> 4.25 us
  transfers between devices with their start and end apart: 6 -> 6, of which waited for: 5 -> 5; matrix products, arithmetic and copies ran while one was open for 3% -> 5% of each run, Pallas kernels for 0% -> 0%
where the time goes in v1:
time: 296 us; the launch traced here: 295 us
  waiting for transfers between devices  159 us (54%)
  blocking collectives  46.3 us (16%)
  matrix products  35.1 us (12%)
  starting transfers between devices  18.9 us (6%)
  local copies, waits for them, and re-layouts  15.6 us (5%)
  between operations  14.7 us (5%)
  other arithmetic  6.02 us (2%)
    psum x1, waiting for transfers between devices, local(): raw = lax.psum(jnp.concatenate([latent_part, rope_part], axis=1), 'seq')  53.3 us
    all_gather x1, waiting for transfers between devices, local(): lax.all_gather(arrived.reshape(total_slots, width), 'seq', axis=0, tiled=...  49.3 us
    reduce_scatter x1, waiting for transfers between devices, local(): summed = lax.psum_scatter(terms, 'seq', scatter_dimension=0, tiled=True)  49.3 us
    all_to_all x1, blocking collectives, local(): lax.all_to_all(outgoing, 'ep', split_axis=0, concat_axis=0, tiled=True)  33.6 us
    dot_general x1, matrix products, expert_terms(): return jnp.dot(hidden, down_matrix, preferred_element_type=jnp.float32)  16 us
    all_gather x1, blocking collectives, local(): older_rot = lax.all_gather(cache_rope[0], 'seq', axis=1, tiled=True)  12.7 us
    all_to_all x1, starting transfers between devices, local(): lax.all_to_all(summed, 'ep', split_axis=0, concat_axis=0, tiled=True)  9.67 us
    all_to_all x1, starting transfers between devices, local(): blocks = lax.all_to_all(blocks, 'seq', split_axis=0, concat_axis=0)  8.91 us
  transfers between devices with their start and end apart: 6, of which 5 were waited for; matrix products, arithmetic and copies ran while one was open for 5% of the time, Pallas kernels for 0%

profile of v1, /device:TPU:1, one launch (start us, length us, event | category | flops | bytes accessed | tf_op | source)
XLA Modules:
  0.0 295.4 jit_solution(15736161494422817048)
XLA Ops:
  7.2 0.8 constant_dynamic-slice_fusion.1
  8.2 0.4 compare_reduce_fusion
  8.8 1.0 fusion.28
  9.8 1.3 convolution_convert_fusion.1
  11.1 0.3 reshape.117
  11.4 33.6 %all_to_all.15 = bf16[32,2,7168]{2,1,0:T(2,128)(2,1)S(1)} all-to-all(bf16[32,2,7168]{2,1,0:T(2,128)(2,1)S(1)} %reshape.117), channel_id=1, replica_groups=mesh['seq'=8,'ep'=32] {'ep'}, dimensions={0} | all-to-all | bytes 1835008 | tf_op jit(solution)/shard_map/all_to_all | solution.py:88
  45.0 1.3 reshape.118
  46.4 49.3 %all-gather.5.cloned.1.call-done = bf16[512,7168]{1,0:T(8,128)(2,1)} async-done(((bf16[64,7168]{1,0:T(8,128)(2,1)}), bf16[512,7168]{1,0:T(8,128)(2,1)}) %all-gather.5.cloned.1.call-update) | async-done | bytes 7340048 | tf_op jit(solution)/shard_map/all_gather | solution.py:89
  95.7 6.2 %fusion.4 = f32[512,256]{1,0:T(8,128)S(1)} fusion(bf16[512,7168]{1,0:T(8,128)(2,1)} %all-gather.5.cloned.1.call-done, bf16[1,7168,256]{2,1,0:T(8,128)(2,1)} %param.19), kind=kOutput, calls=%fused_computation.7 | convolution fusion | flops 1879048192 | bytes 11534336 | tf_op jit(solution)/shard_map/dot_general | solution.py:44
  101.9 16.0 %convolution_convert_fusion = bf16[512,7168]{1,0:T(8,128)(2,1)} fusion(bf16[1,256,7168]{2,1,0:T(8,128)(2,1)} %param.21, bf16[512,7168]{1,0:T(8,128)(2,1)} %all-gather.5.cloned.1.call-done, bf16[1,7168,256]{2,1,0:T(8,128)(2,1)} %param.20, f32[512,256]{1,0:T(8,128)S(1)} %fusion.4), kind=kOutput, calls=%fused_computation | convolution fusion | flops 3762552832 | bytes 22544384 | tf_op jit(solution)/shard_map/dot_general | solution.py:47
  118.0 49.3 %reduce-scatter.2.cloned.1.call-done = bf16[64,7168]{1,0:T(8,128)(2,1)} async-done(((bf16[512,7168]{1,0:T(8,128)(2,1)}), bf16[64,7168]{1,0:T(8,128)(2,1)}) %reduce-scatter.2.cloned.1.call-update) | async-done | bytes 917520 | tf_op jit(solution)/shard_map/reduce_scatter | solution.py:104
  167.2 3.1 %reshape.119 = bf16[32,2,7168]{2,1,0:T(2,128)(2,1)} reshape(bf16[64,7168]{1,0:T(8,128)(2,1)} %reduce-scatter.2.cloned.1.call-done) | data formatting | bytes 1835008 | tf_op jit(solution)/shard_map/reshape | solution.py:105
  170.3 9.7 %all-to-all-start.1 = ((bf16[32,2,7168]{2,1,0:T(2,128)(2,1)}), bf16[32,2,7168]{2,1,0:T(2,128)(2,1)S(1)}, u32[]{:S(2)}, u32[]{:S(2)}) async-start(bf16[32,2,7168]{2,1,0:T(2,128)(2,1)} %reshape.119), calls=%async_computation.2 | async-start | bytes 1835008 | tf_op jit(solution)/shard_map/all_to_all | solution.py:106
  180.0 0.2 all-gather.7.cloned.1.call-start
  180.2 0.5 all-gather.7.cloned.1.call-update
  181.1 0.4 reshape_squeeze.6
  182.2 12.7 %all-gather.1 = bf16[1,64,1024]{2,1,0:T(8,128)(2,1)S(1)} all-gather(bf16[1,64,128]{2,1,0:T(8,128)(2,1)S(1)} %copy-done.6), channel_id=3, replica_groups=mesh['seq'=8,'ep'=32] {'seq'}, dimensions={2}, use_global_device_ids=true | all-gather | bytes 147456 | tf_op jit(solution)/shard_map/all_gather | solution.py:91
  194.8 0.6 negate_power_fusion
  195.4 0.5 add_convert_fusion
  196.1 1.8 fusion.26
  197.8 4.2 %all-to-all-done.1 = bf16[32,2,7168]{2,1,0:T(2,128)(2,1)S(1)} async-done(((bf16[32,2,7168]{2,1,0:T(2,128)(2,1)}), bf16[32,2,7168]{2,1,0:T(2,128)(2,1)S(1)}, u32[]{:S(2)}, u32[]{:S(2)}) %all-to-all-start.1) | async-done | bytes 917536 | tf_op jit(solution)/shard_map/all_to_all | solution.py:106
  202.0 0.3 reshape.120
  202.4 0.5 fusion
  202.8 0.6 constant_dynamic-update-slice_fusion.7
  203.4 0.6 constant_dynamic-update-slice_fusion.6
  204.0 0.6 constant_dynamic-update-slice_fusion.5
  204.6 0.6 constant_dynamic-update-slice_fusion.4
  205.2 0.6 constant_dynamic-update-slice_fusion.3
  205.8 0.6 constant_dynamic-update-slice_fusion.2
  206.4 0.6 constant_dynamic-update-slice_fusion.1
  207.0 0.6 constant_dynamic-update-slice_fusion
  207.6 8.9 %all-to-all-start.2 = ((bf16[8,4,896]{2,1,0:T(4,128)(2,1)}), bf16[8,4,896]{2,1,0:T(4,128)(2,1)}, u32[]{:S(2)}, u32[]{:S(2)}) async-start(bf16[8,4,896]{2,1,0:T(4,128)(2,1)} %constant_dynamic-update-slice_fusion), calls=%async_computation.3 | async-start | bytes 114688 | tf_op jit(solution)/shard_map/all_to_all | solution.py:115
  216.6 2.8 fusion.58
  219.3 2.1 all-to-all-done.2
  221.5 1.5 reshape.121
  222.9 1.1 fusion.61
  224.0 1.1 fusion.60
  225.1 0.7 pad_maximum_fusion
  225.8 0.5 fusion.6
  226.2 1.5 broadcast_in_dim_reshape.6
  227.7 53.3 %all-reduce.2.cloned.1.call-done = f32[32,576]{1,0:T(8,128)} async-done(((f32[32,576]{1,0:T(8,128)}), f32[32,576]{1,0:T(8,128)}) %all-reduce.2.cloned.1.call-update) | async-done | bytes 73744 | tf_op jit(solution)/shard_map/psum | solution.py:121
  281.0 1.0 multiply_reduce_fusion
  282.1 1.1 fusion.57
  283.1 1.0 fusion.44
  284.1 1.1 fusion.59
  285.3 2.0 convolution_multiply_fusion
  287.3 0.3 fusion.9
  287.6 1.2 broadcast_in_dim_reshape.7
  (41 shorter events, 1.0 us)
Async XLA Ops:
  7.2 216.9 %copy-start = (bf16[896,512]{1,0:T(8,128)(2,1)S(1)}, bf16[896,512]{1,0:T(8,128)(2,1)}, u32[]{:S(2)}) copy-start(bf16[896,512]{1,0:T(8,128)(2,1)} %param.22) | copy-start | bytes 2752516
  7.2 88.5 %all-gather.5.cloned.1.call-start = ((), (), s32[]{:S(2)}) async-start(), calls=%async_computation.4 | async-start | bytes 8257536 | tf_op jit(solution)/shard_map/all_gather | solution.py:89
  46.3 120.9 %reduce-scatter.2.cloned.1.call-start = ((), (), s32[]{:S(2)}) async-start(), calls=%async_computation.5 | async-start | bytes 8257536 | tf_op jit(solution)/shard_map/reduce_scatter | solution.py:104
  117.9 62.8 %copy-start.7 = (f32[1,32,8]{1,2,0:T(8,128)S(1)}, f32[1,32,8]{1,2,0:T(8,128)}, u32[]{:S(2)}) copy-start(f32[1,32,8]{1,2,0:T(8,128)} %param.18) | copy-start | bytes 3076
  117.9 63.0 %copy-start.5 = (bf16[1,4,8192]{2,1,0:T(4,128)(2,1)S(1)}, bf16[1,4,8192]{2,1,0:T(4,128)(2,1)}, u32[]{:S(2)}) copy-start(bf16[1,4,8192]{2,1,0:T(4,128)(2,1)} %param.29) | copy-start | bytes 196612
  117.9 63.1 %copy-start.2 = (bf16[1,4,65536]{2,1,0:T(4,128)(2,1)S(1)}, bf16[1,4,65536]{2,1,0:T(4,128)(2,1)}, u32[]{:S(2)}) copy-start(bf16[1,4,65536]{2,1,0:T(4,128)(2,1)} %param.28) | copy-start | bytes 1572868
  118.0 64.2 %copy-start.6 = (bf16[1,64,128]{2,1,0:T(8,128)(2,1)S(1)}, bf16[1,64,128]{2,1,0:T(8,128)(2,1)}, u32[]{:S(2)}) copy-start(bf16[1,64,128]{2,1,0:T(8,128)(2,1)} %param.27) | copy-start | bytes 49156
  170.3 32.1 %copy-start.3 = (bf16[1,4,7168]{2,1,0:T(4,128)(2,1)S(1)}, bf16[1,4,7168]{2,1,0:T(4,128)(2,1)}, u32[]{:S(2)}) copy-start(bf16[1,4,7168]{2,1,0:T(4,128)(2,1)} %param.15) | copy-start | bytes 172036
  170.3 31.7 %all-to-all-start.1 = ((bf16[32,2,7168]{2,1,0:T(2,128)(2,1)}), bf16[32,2,7168]{2,1,0:T(2,128)(2,1)S(1)}, u32[]{:S(2)}, u32[]{:S(2)}) async-start(bf16[32,2,7168]{2,1,0:T(2,128)(2,1)} %reshape.119), calls=%async_computation.2 | async-start | bytes 1835008 | tf_op jit(solution)/shard_map/all_to_all | solution.py:106
  180.0 36.6 %all-gather.7.cloned.1.call-start = ((), (), s32[]{:S(2)}) async-start(), calls=%async_computation.7 | async-start | bytes 1179648 | tf_op jit(solution)/shard_map/all_gather | solution.py:90
  181.1 16.8 %copy-start.1 = (bf16[512,64]{1,0:T(8,128)(2,1)}, bf16[512,64]{1,0:T(8,128)(2,1)S(1)}, u32[]{:S(2)}) copy-start(bf16[512,64]{1,0:T(8,128)(2,1)S(1)} %reshape_squeeze.7) | copy-start | bytes 196612
  207.6 13.8 %all-to-all-start.2 = ((bf16[8,4,896]{2,1,0:T(4,128)(2,1)}), bf16[8,4,896]{2,1,0:T(4,128)(2,1)}, u32[]{:S(2)}, u32[]{:S(2)}) async-start(bf16[8,4,896]{2,1,0:T(4,128)(2,1)} %constant_dynamic-update-slice_fusion), calls=%async_computation.3 | async-start | bytes 114688 | tf_op jit(solution)/shard_map/all_to_all | solution.py:115
  216.5 65.5 %copy-start.8 = (f32[512]{0:T(512)S(1)}, f32[512]{0:T(512)}, u32[]{:S(2)}) copy-start(f32[512]{0:T(512)} %param.24) | copy-start | bytes 6148
  216.5 64.5 %all-reduce.2.cloned.1.call-start = ((), (), s32[]{:S(2)}) async-start(), calls=%async_computation.6 | async-start | bytes 163840 | tf_op jit(solution)/shard_map/psum | solution.py:121
  281.0 6.3 %copy-start.4 = (f32[32,576]{1,0:T(8,128)S(1)}, f32[32,576]{1,0:T(8,128)}, u32[]{:S(2)}) copy-start(f32[32,576]{1,0:T(8,128)} %all-reduce.2.cloned.1.call-done) | copy-start | bytes 221188
Sparse Core Ops, SparseCore 0:
  46.5 49.1 all-gather.4
  118.0 49.1 reduce-scatter.1
  182.7 26.2 all-gather.6
  225.9 55.0 all-reduce.1
